TPU v7x, 32 devices: a whole 2x2x4 slice. The times are simulated.
32 devices in a mesh: parts: 2 (over y), gx: 8 (over z, x), gy: 2 (over core).
Axes of the slice: x: 2, y: 2, z: 4, core: 2. Of those that a mesh axis runs over, the one named last changes fastest.
Arguments:
- conc: float32 [12, 256, 2, 256], P(None, ('parts', 'gx'), None, 'gy'), parts along dimension 1, may hold values from 0.1 to 2
- sens: float32 [8, 12, 256, 2, 256], P(None, None, ('parts', 'gx'), None, 'gy'), parts along dimension 2, may hold values from -6 to 6
- vel_x: float32 [256, 2, 256], P(('parts', 'gx'), None, 'gy'), parts along dimension 0, may hold values from 0.3 to 1
- vel_y: float32 [256, 2, 256], P(('parts', 'gx'), None, 'gy'), parts along dimension 0, may hold values from 0.3 to 1
- up_x: int32 [256, 2, 256], P(('parts', 'gx'), None, 'gy'), parts along dimension 0, may hold values 0 or 1
- up_y: int32 [256, 2, 256], P(('parts', 'gx'), None, 'gy'), parts along dimension 0, may hold values 0 or 1
- sorb_zone: int32 [256, 2, 256], P(('parts', 'gx'), None, 'gy'), parts along dimension 0, may hold values from 0 to 2
- rate_zone: int32 [256, 2, 256], P(('parts', 'gx'), None, 'gy'), parts along dimension 0, may hold values from 0 to 7
- param_values: float32 [8], replicated, may hold values from 0.1 to 0.5
- mol_diff: float32 [12], replicated, may hold values from 0.02 to 0.2
- sorb_cap: float32 [12], replicated, may hold values from 0.2 to 2
- rate_table: float32 [8, 3], replicated, may hold values from 0.5 to 2
- exch_matrix: float32 [12, 12], replicated, may hold values from -1.75 to 1.75
- stoich: float32 [12, 3], replicated, may hold values from -2 to 2
Outputs:
- conc_out: float32 [12, 256, 2, 256], P(None, ('parts', 'gx'), None, 'gy'), parts along dimension 1
- sens_out: float32 [8, 12, 256, 2, 256], P(None, None, ('parts', 'gx'), None, 'gy'), parts along dimension 2
There are 2 independent parts, one for each index of `parts`. A program takes and returns all parts, laid end to end along the dimension named above; an argument that names none is the same for every part. Nothing has to cross between parts.
All inputs are finite; a program needn't handle non-finite values. No bound on the sum of `up_x` or of `up_y` on one device may be relied on, other than what follows from the above.
Results may differ from a plain program's by a relative error of at most 0.000078.
Values sent between devices are 32-bit elements; how exact they have to be, the bound alone decides.
A program may use at most 64 MiB of HBM per device.

v0:
```python
import functools
import jax
import jax.numpy as jnp
from jax import lax
from jax.experimental import pallas as pl
from jax.experimental.pallas import tpu as pltpu
from jax.sharding import PartitionSpec as P

NC = 12
NP = 8
NK = NP + 1
NR = 3
SZONES = 3
RZONES = 8
GROUPS = 3
PER = NC // GROUPS
HALO = 2 * PER * NK

DISP_STEP = 0.25
COURANT = 0.2
REACT_STEP = 0.2
PAD = 8


def kernel(
    rows,
    lanes,
    conc_ref,
    sens_ref,
    vx_ref,
    vy_ref,
    ux_ref,
    uy_ref,
    sz_ref,
    rz_ref,
    p_ref,
    mol_ref,
    cap_ref,
    table_ref,
    exch_ref,
    stoich_ref,
    conc_out,
    sens_out,
    sta,
    stb,
    xsend,
    xrecv,
    ysend,
    yrecv,
    vsend,
    vrecv,
    fields,
    load_sem,
    xs_sem,
    xr_sem,
    ys_sem,
    yr_sem,
    vs_sem,
    vr_sem,
):
    gx = lax.axis_index("gx")
    gy = lax.axis_index("gy")
    ngx = lax.axis_size("gx")
    has_lo = gx > 0
    has_hi = gx < ngx - 1
    body = pl.ds(PAD, rows)

    loads = [pltpu.make_async_copy(conc_ref, sta.at[0, :, body, :], load_sem.at[0])]
    loads.append(pltpu.make_async_copy(sens_ref, sta.at[pl.ds(1, NP), :, body, :], load_sem.at[1]))
    for copy in loads:
        copy.start()

    barrier = pltpu.get_barrier_semaphore()
    pl.semaphore_signal(barrier, inc=1, device_id={"gy": 1 - gy})

    @pl.when(has_lo)
    def _():
        pl.semaphore_signal(barrier, inc=1, device_id={"gx": gx - 1})

    @pl.when(has_hi)
    def _():
        pl.semaphore_signal(barrier, inc=1, device_id={"gx": gx + 1})

    lane = lax.broadcasted_iota(jnp.int32, (rows, lanes), 1)
    row = lax.broadcasted_iota(jnp.int32, (rows, lanes), 0)
    even = (row % 2) == 0
    inner_lane = jnp.where(gy == 0, lanes - 1, 0)
    first = lane == 0
    last = lane == lanes - 1
    inner = lane == inner_lane

    vx = vx_ref[...]
    vy = vy_ref[...]
    ux = ux_ref[...].astype(jnp.float32)
    uy = uy_ref[...].astype(jnp.float32)
    vsend[0:2, :] = vx[0:2]
    vsend[2:4, :] = ux[0:2]

    @pl.when(jnp.logical_not(has_lo))
    def _():
        xrecv[:, 0] = jnp.zeros_like(xrecv[:, 0])

    @pl.when(jnp.logical_not(has_hi))
    def _():
        xrecv[:, 1] = jnp.zeros_like(xrecv[:, 1])
        vrecv[...] = jnp.zeros_like(vrecv)


    def lo_copy(stage):
        return pltpu.make_async_remote_copy(
            src_ref=xsend.at[stage, 0],
            dst_ref=xrecv.at[stage, 1],
            send_sem=xs_sem.at[stage, 0],
            recv_sem=xr_sem.at[stage, 1],
            device_id={"gx": gx - 1},
        )

    def hi_copy(stage):
        return pltpu.make_async_remote_copy(
            src_ref=xsend.at[stage, 1],
            dst_ref=xrecv.at[stage, 0],
            send_sem=xs_sem.at[stage, 1],
            recv_sem=xr_sem.at[stage, 0],
            device_id={"gx": gx + 1},
        )

    def y_copy(stage):
        return pltpu.make_async_remote_copy(
            src_ref=ysend.at[stage],
            dst_ref=yrecv.at[stage],
            send_sem=ys_sem.at[stage],
            recv_sem=yr_sem.at[stage],
            device_id={"gy": 1 - gy},
        )

    v_copy = pltpu.make_async_remote_copy(
        src_ref=vsend,
        dst_ref=vrecv,
        send_sem=vs_sem,
        recv_sem=vr_sem,
        device_id={"gx": gx - 1},
    )

    def send_x(src, stage):
        def step(g, carry):
            for j in range(PER):
                c = g * PER + j
                for k in range(NK):
                    off = 2 * (j * NK + k)
                    xsend[stage, 0, g, off : off + 2, :] = src[k, c, PAD : PAD + 2, :]
                    xsend[stage, 1, g, off : off + 2, :] = src[k, c, PAD + rows - 2 : PAD + rows, :]
            return carry

        lax.fori_loop(0, GROUPS, step, 0)

        @pl.when(has_lo)
        def _():
            lo_copy(stage).start()

        @pl.when(has_hi)
        def _():
            hi_copy(stage).start()

    def send_y(src, stage, start):
        def step(g, acc):
            for j in range(PER):
                c = g * PER + j
                for k in range(NK):
                    slot = c * NK + k
                    shift = lax.rem(slot - inner_lane + lanes, lanes)
                    moved = pltpu.roll(src[k, c, body, :], shift, 1)
                    acc = jnp.where(lane == slot, moved, acc)
            return acc

        ysend[stage] = lax.fori_loop(0, GROUPS, step, start)
        y_copy(stage).start()

    def receive(dst, stage):
        @pl.when(has_lo)
        def _():
            hi_copy(stage).wait_recv()

        @pl.when(has_hi)
        def _():
            lo_copy(stage).wait_recv()

        y_copy(stage).wait_recv()

        def step(g, carry):
            for j in range(PER):
                c = g * PER + j
                for k in range(NK):
                    off = 2 * (j * NK + k)
                    dst[k, c, PAD - 2 : PAD, :] = xrecv[stage, 0, g, off : off + 2, :]
                    dst[k, c, PAD + rows : PAD + rows + 2, :] = xrecv[stage, 1, g, off : off + 2, :]
            return carry

        lax.fori_loop(0, GROUPS, step, 0)

    def y_halo(stage, slot):
        return pltpu.roll(yrecv[stage], lax.rem(inner_lane - slot + lanes, lanes), 1)

    def disperse(src, stage, put):
        def step(c, carry):
            m = DISP_STEP * mol_ref[c]
            cx = fields[0] + m
            cy = fields[1] + m
            c0 = 1.0 - 2.0 * cx - 2.0 * cy - m
            cyl = jnp.where(first, 0.0, cy)
            cyh = jnp.where(last, 0.0, cy)
            cyi = jnp.where(inner, cy, 0.0)
            for k in range(NK):
                v = src[k, c, body, :]
                sx = src[k, c, PAD - 2 : PAD - 2 + rows, :] + src[k, c, PAD + 2 : PAD + 2 + rows, :]
                other = jnp.where(
                    even,
                    src[k, c, PAD + 1 : PAD + 1 + rows, :],
                    src[k, c, PAD - 1 : PAD - 1 + rows, :],
                )
                yl = pltpu.roll(v, 1, 1)
                yh = pltpu.roll(v, lanes - 1, 1)
                yi = y_halo(stage, c * NK + k)
                out = c0 * v + cx * sx + m * other + cyl * yl + cyh * yh + cyi * yi
                if k == 0:
                    lap_x = sx - 2.0 * v
                    lap_y = (
                        jnp.where(first, 0.0, yl)
                        + jnp.where(last, 0.0, yh)
                        + jnp.where(inner, yi, 0.0)
                        - 2.0 * v
                    )
                if k == 1:
                    out = out + DISP_STEP * vx_ref[...] * lap_x
                if k == 2:
                    out = out + DISP_STEP * vy_ref[...] * lap_y
                put(k, c, out)
            return carry

        lax.fori_loop(0, NC, step, 0)

    def put_stb(k, c, out):
        stb[k, c, body, :] = out

    def put_out(k, c, out):
        if k == 0:
            conc_out[c] = out
        else:
            sens_out[k - 1, c] = out

    fields[0] = DISP_STEP * p_ref[0] * vx
    fields[1] = DISP_STEP * p_ref[1] * vy

    y_start = jnp.where(
        lane == NK * NC,
        pltpu.roll(vy, lax.rem(NK * NC - inner_lane + lanes, lanes), 1),
        pltpu.roll(uy, lax.rem(NK * NC + 1 - inner_lane + lanes, lanes), 1),
    )

    for copy in loads:
        copy.wait()

    count = 1 + has_lo.astype(jnp.int32) + has_hi.astype(jnp.int32)
    pl.semaphore_wait(barrier, count)

    @pl.when(has_lo)
    def _():
        v_copy.start()

    send_x(sta, 0)
    send_y(sta, 0, y_start)
    receive(sta, 0)
    disperse(sta, 0, put_stb)

    send_x(stb, 1)
    send_y(stb, 1, jnp.zeros((rows, lanes), jnp.float32))

    @pl.when(has_hi)
    def _():
        v_copy.wait_recv()

    vx_next = jnp.concatenate([vx[2:], vrecv[0:2, :]], 0)
    ux_next = jnp.concatenate([ux[2:], vrecv[2:4, :]], 0)
    open_hi = gy == 0
    edge = jnp.where(open_hi, lanes - 1, 0)
    vy_in = pltpu.roll(yrecv[0], lax.rem(edge - NK * NC + lanes, lanes), 1)
    uy_in = pltpu.roll(yrecv[0], lax.rem(edge - NK * NC - 1 + lanes, lanes), 1)
    keep = jnp.where(open_hi, 1.0, 0.0)
    vy_next = jnp.where(last, vy_in * keep, pltpu.roll(vy, lanes - 1, 1))
    uy_next = jnp.where(last, uy_in * keep, pltpu.roll(uy, lanes - 1, 1))
    axl = vx * ux
    axh = vx_next * (1.0 - ux_next)
    ayl = vy * uy
    ayh = vy_next * (1.0 - uy_next)
    fields[2] = vx_next * ux_next + vx * (1.0 - ux) + vy_next * uy_next + vy * (1.0 - uy)
    fields[3] = axl
    fields[4] = axh
    fields[5] = jnp.where(first, 0.0, ayl)
    fields[6] = jnp.where(last, 0.0, ayh)
    fields[7] = jnp.where(inner, keep * ayh + (1.0 - keep) * ayl, 0.0)
    sorb_zone = sz_ref[...]
    sorb = jnp.zeros((rows, lanes), jnp.float32)
    for z in range(SZONES):
        sorb = jnp.where(sorb_zone == z, p_ref[5 + z], sorb)
    fields[8] = sorb
    rate_zone = rz_ref[...]
    for r in range(NR):
        rate = jnp.zeros((rows, lanes), jnp.float32)
        for z in range(RZONES):
            rate = jnp.where(rate_zone == z, table_ref[r, z], rate)
        fields[9 + r] = rate

    receive(stb, 1)

    def advect(c, carry):
        cap = cap_ref[c]
        retard = 1.0 + fields[8] * cap
        scale = COURANT / retard
        for k in range(NK):
            v = stb[k, c, body, :]
            div = (
                fields[2] * v
                - fields[3] * stb[k, c, PAD - 2 : PAD - 2 + rows, :]
                - fields[4] * stb[k, c, PAD + 2 : PAD + 2 + rows, :]
                - fields[5] * pltpu.roll(v, 1, 1)
                - fields[6] * pltpu.roll(v, lanes - 1, 1)
                - fields[7] * y_halo(1, c * NK + k)
            )
            out = v - scale * div
            if k == 0:
                extra = cap * div * (scale / retard)
            if k >= 6:
                out = out + jnp.where(sz_ref[...] == k - 6, extra, 0.0)
            sta[k, c, body, :] = out
        return carry

    lax.fori_loop(0, NC, advect, 0)

    half = rows // 2
    for h in range(2):
        part = pl.ds(PAD + h * half, half)
        fpart = pl.ds(h * half, half)
        s = [sta[0, c, part, :] for c in range(2 * NR)]
        source = [fields[9 + r, fpart, :] * s[2 * r] * s[2 * r + 1] for r in range(NR)]

        def mix(k, v, q):
            for c in range(NC):
                acc = exch_ref[c, 0] * v[0]
                for d in range(1, NC):
                    acc = acc + exch_ref[c, d] * v[d]
                for r in range(NR):
                    acc = acc + stoich_ref[r, c] * q[r]
                sta[k, c, part, :] = v[c] + REACT_STEP * acc

        def tangent(k, carry):
            v = [sta[k, c, part, :] for c in range(NC)]
            q = []
            for r in range(NR):
                factor = p_ref[2 + r] * fields[9 + r, fpart, :]
                flag = jnp.where(k == 3 + r, 1.0, 0.0)
                q.append(factor * (s[2 * r + 1] * v[2 * r] + s[2 * r] * v[2 * r + 1]) + flag * source[r])
            mix(k, v, q)
            return carry

        lax.fori_loop(1, NK, tangent, 0)
        mix(0, [sta[0, c, part, :] for c in range(NC)], [p_ref[2 + r] * source[r] for r in range(NR)])

    send_x(sta, 2)
    send_y(sta, 2, jnp.zeros((rows, lanes), jnp.float32))
    receive(sta, 2)
    disperse(sta, 2, put_out)

    for stage in range(3):
        y_copy(stage).wait_send()

    @pl.when(has_lo)
    def _():
        for stage in range(3):
            lo_copy(stage).wait_send()
        v_copy.wait_send()

    @pl.when(has_hi)
    def _():
        for stage in range(3):
            hi_copy(stage).wait_send()


def on_device(
    conc,
    sens,
    vel_x,
    vel_y,
    up_x,
    up_y,
    sorb_zone,
    rate_zone,
    param_values,
    mol_diff,
    sorb_cap,
    rate_table,
    exch_matrix,
    stoich,
):
    nx, layers, ny = vel_x.shape
    rows = nx * layers
    flat = lambda a: a.reshape(a.shape[:-3] + (rows, ny))
    vmem = pl.BlockSpec(memory_space=pltpu.VMEM)
    smem = pl.BlockSpec(memory_space=pltpu.SMEM)
    hbm = pl.BlockSpec(memory_space=pl.ANY)
    f32 = jnp.float32
    state = (NK, NC, rows + 2 * PAD, ny)
    conc_out, sens_out = pl.pallas_call(
        functools.partial(kernel, rows, ny),
        out_shape=(
            jax.ShapeDtypeStruct((NC, rows, ny), f32),
            jax.ShapeDtypeStruct((NP, NC, rows, ny), f32),
        ),
        in_specs=[hbm, hbm] + [vmem] * 6 + [smem] * 6,
        out_specs=(vmem, vmem),
        scratch_shapes=[
            pltpu.VMEM(state, f32),
            pltpu.VMEM(state, f32),
            pltpu.VMEM((3, 2, GROUPS, HALO, ny), f32),
            pltpu.VMEM((3, 2, GROUPS, HALO, ny), f32),
            pltpu.VMEM((3, rows, ny), f32),
            pltpu.VMEM((3, rows, ny), f32),
            pltpu.VMEM((8, ny), f32),
            pltpu.VMEM((8, ny), f32),
            pltpu.VMEM((12, rows, ny), f32),
            pltpu.SemaphoreType.DMA((2,)),
            pltpu.SemaphoreType.DMA((3, 2)),
            pltpu.SemaphoreType.DMA((3, 2)),
            pltpu.SemaphoreType.DMA((3,)),
            pltpu.SemaphoreType.DMA((3,)),
            pltpu.SemaphoreType.DMA,
            pltpu.SemaphoreType.DMA,
        ],
        compiler_params=pltpu.CompilerParams(
            collective_id=0, has_side_effects=True, vmem_limit_bytes=62 * 1024 * 1024
        ),
    )(
        flat(conc),
        flat(sens),
        flat(vel_x),
        flat(vel_y),
        flat(up_x),
        flat(up_y),
        flat(sorb_zone),
        flat(rate_zone),
        param_values,
        mol_diff,
        sorb_cap,
        jnp.transpose(rate_table),
        exch_matrix,
        jnp.transpose(stoich),
    )
    return conc_out.reshape(conc.shape), sens_out.reshape(sens.shape)


def solution(mesh):
    cell = P(("parts", "gx"), None, "gy")
    outs = (P(None, ("parts", "gx"), None, "gy"), P(None, None, ("parts", "gx"), None, "gy"))
    return jax.shard_map(
        on_device,
        mesh=mesh,
        in_specs=outs + (cell,) * 6 + (P(),) * 6,
        out_specs=outs,
        check_vma=False,
    )
```

profile of v0, /device:TPU:17, one launch (start us, length us, event | category | flops | bytes accessed | tf_op | source)
XLA Modules:
  0.0 38.6 jit_solution(1800420861618198748)
XLA Ops:
  0.6 33.7 %shard_map.149 = (f32[12,32,128]{2,1,0:T(8,128)}, f32[8,12,32,128]{3,2,1,0:T(8,128)}) custom-call(f32[12,32,128]{2,1,0:T(8,128)} %bitcast.15, f32[8,12,32,128]{3,2,1,0:T(8,128)} %bitcast.13, f32[32,128]{1,0:T(8,128)} %bitcast.16, f32[32,128]{1,0:T(8,128)} %bitcast.17, s32[32,128]{1,0:T(8,128)} %bitcast.18, s32[32,128]{1,0:T(8,128)} %bitcast.19, ...), custom_call_target="tpu_custom_call" | custom-call | tf_op jit(solution)/shard_map/pallas_call | solution.py:411
  34.4 1.6 %copy.18 = f32[12,16,2,128]{3,2,1,0:T(2,128)} copy(f32[12,16,2,128]{3,2,1,0:T(2,128)} %bitcast.14) | data formatting | bytes 393216
  36.0 2.7 %copy.19 = f32[8,12,16,2,128]{4,3,2,1,0:T(2,128)} copy(f32[8,12,16,2,128]{4,3,2,1,0:T(2,128)} %bitcast.12) | data formatting | bytes 3145728
where the time goes:
time: 38.9 us; the launch traced here: 38.6 us
  Pallas kernels  33.7 us (87%)
  local copies, waits for them, and re-layouts  4.28 us (11%)
  between operations  0.64 us (2%)
    pallas_call x1, Pallas kernels, on_device(): pl.pallas_call(functools.partial(kernel, rows, ny), out_shape=(jax.ShapeD...  33.7 us
    unnamed x2, local copies, waits for them, and re-layouts  4.28 us

commit v1 on v0

v1 whole, which is shorter than its diff:
```python
import functools
import jax
import jax.numpy as jnp
from jax import lax
from jax.experimental import pallas as pl
from jax.experimental.pallas import tpu as pltpu
from jax.sharding import PartitionSpec as P

NC = 12
NP = 8
NK = NP + 1
NR = 3
SZONES = 3
RZONES = 8

DISP_STEP = 0.25
COURANT = 0.2
REACT_STEP = 0.2

BASE = 12
EXT = 8
HALO = 6


def kernel(
    rows,
    lanes,
    conc_ref,
    sens_ref,
    vx_ref,
    vy_ref,
    ux_ref,
    uy_ref,
    sz_ref,
    rz_ref,
    p_ref,
    mol_ref,
    cap_ref,
    table_ref,
    exch_ref,
    stoich_ref,
    conc_out,
    sens_out,
    inbuf,
    outbuf,
    sta,
    stb,
    xsend,
    xrecv,
    ysend,
    yrecv,
    fsend,
    frecv,
    cells,
    disp,
    adv,
    scale,
    rates,
    state,
    extra_d,
    extra_a,
    load_sem,
    store_sem,
    xs_sem,
    xr_sem,
    ys_sem,
    yr_sem,
    fs_sem,
    fr_sem,
):
    gx = lax.axis_index("gx")
    gy = lax.axis_index("gy")
    ngx = lax.axis_size("gx")
    has_lo = gx > 0
    has_hi = gx < ngx - 1
    wide = rows + 2 * (BASE - EXT)
    f32 = jnp.float32

    def load(k):
        return pltpu.make_async_copy(sens_ref.at[k - 1], inbuf.at[k], load_sem.at[k])

    load_first = pltpu.make_async_copy(conc_ref, inbuf.at[0], load_sem.at[0])
    load_first.start()
    for k in range(1, NK):
        load(k).start()

    barrier = pltpu.get_barrier_semaphore()
    pl.semaphore_signal(barrier, inc=1, device_id={"gy": 1 - gy})

    @pl.when(has_lo)
    def _():
        pl.semaphore_signal(barrier, inc=1, device_id={"gx": gx - 1})

    @pl.when(has_hi)
    def _():
        pl.semaphore_signal(barrier, inc=1, device_id={"gx": gx + 1})

    own = (
        vx_ref[...],
        vy_ref[...],
        ux_ref[...].astype(f32),
        uy_ref[...].astype(f32),
        sz_ref[...].astype(f32),
        rz_ref[...].astype(f32),
    )
    for f in range(6):
        fsend[0, HALO * f : HALO * (f + 1), :] = own[f][0:HALO]
        fsend[1, HALO * f : HALO * (f + 1), :] = own[f][rows - HALO : rows]
        cells[f, BASE : BASE + rows, :] = own[f]

    @pl.when(jnp.logical_not(has_lo))
    def _():
        xrecv[:, 0] = jnp.zeros_like(xrecv[:, 0])
        frecv[0] = jnp.zeros_like(frecv[0])

    @pl.when(jnp.logical_not(has_hi))
    def _():
        xrecv[:, 1] = jnp.zeros_like(xrecv[:, 1])
        frecv[1] = jnp.zeros_like(frecv[1])

    def x_copy(k, side):
        return pltpu.make_async_remote_copy(
            src_ref=xsend.at[k, side],
            dst_ref=xrecv.at[k, 1 - side],
            send_sem=xs_sem.at[k, side],
            recv_sem=xr_sem.at[k, 1 - side],
            device_id={"gx": gx - 1 if side == 0 else gx + 1},
        )

    def f_copy(side):
        return pltpu.make_async_remote_copy(
            src_ref=fsend.at[side],
            dst_ref=frecv.at[1 - side],
            send_sem=fs_sem.at[side],
            recv_sem=fr_sem.at[1 - side],
            device_id={"gx": gx - 1 if side == 0 else gx + 1},
        )

    def y_copy(stage, k):
        return pltpu.make_async_remote_copy(
            src_ref=ysend.at[stage, k],
            dst_ref=yrecv.at[stage, k],
            send_sem=ys_sem.at[stage, k],
            recv_sem=yr_sem.at[stage, k],
            device_id={"gy": 1 - gy},
        )

    count = 1 + has_lo.astype(jnp.int32) + has_hi.astype(jnp.int32)
    pl.semaphore_wait(barrier, count)

    @pl.when(has_lo)
    def _():
        f_copy(0).start()

    @pl.when(has_hi)
    def _():
        f_copy(1).start()

    def send(k):
        for c in range(NC):
            xsend[k, 0, HALO * c : HALO * (c + 1), :] = inbuf[k, c, 0:HALO, :]
            xsend[k, 1, HALO * c : HALO * (c + 1), :] = inbuf[k, c, rows - HALO : rows, :]

        @pl.when(has_lo)
        def _():
            x_copy(k, 0).start()

        @pl.when(has_hi)
        def _():
            x_copy(k, 1).start()

    load_first.wait()
    send(0)

    def send_step(k, carry):
        load(k).wait()
        send(k)
        return carry

    lax.fori_loop(1, NK, send_step, 0)

    @pl.when(has_lo)
    def _():
        f_copy(1).wait_recv()

    @pl.when(has_hi)
    def _():
        f_copy(0).wait_recv()

    for f in range(6):
        cells[f, BASE - HALO : BASE, :] = frecv[0, HALO * f : HALO * (f + 1), :]
        cells[f, BASE + rows : BASE + rows + HALO, :] = frecv[1, HALO * f : HALO * (f + 1), :]

    lane = lax.broadcasted_iota(jnp.int32, (wide, lanes), 1)
    row = lax.broadcasted_iota(jnp.int32, (wide, lanes), 0)
    even = (row % 2) == 0
    inner_lane = jnp.where(gy == 0, lanes - 1, 0)
    first = lane == 0
    last = lane == lanes - 1
    inner = lane == inner_lane
    margin = BASE - EXT
    lo_ok = jnp.where(has_lo, 1.0, 0.0)
    hi_ok = jnp.where(has_hi, 1.0, 0.0)
    valid = jnp.where(row < margin, lo_ok, jnp.where(row >= margin + rows, hi_ok, 1.0))
    ext = pl.ds(EXT, wide)

    fx = DISP_STEP * p_ref[0] * cells[0, ext, :]
    fy = DISP_STEP * p_ref[1] * cells[1, ext, :]
    sorb = jnp.zeros((wide, lanes), f32)
    for z in range(SZONES):
        sorb = jnp.where(cells[4, ext, :] == float(z), p_ref[5 + z], sorb)

    def coefficients(c, carry):
        m = DISP_STEP * mol_ref[c]
        cx = (fx + m) * valid
        cy = (fy + m) * valid
        cm = m * valid
        disp[0, c] = valid - 2.0 * cx - 2.0 * cy - cm
        disp[1, c] = cx
        disp[2, c] = cm
        disp[3, c] = jnp.where(first, 0.0, cy)
        disp[4, c] = jnp.where(last, 0.0, cy)
        disp[5, c] = jnp.where(inner, cy, 0.0)
        scale[c] = valid * COURANT / (1.0 + sorb * cap_ref[c])
        for stage in range(2):
            extra_d[stage, 0, c] = jnp.zeros((wide, lanes), f32)
        return carry

    lax.fori_loop(0, NC, coefficients, 0)
    for r in range(NR):
        rate = jnp.zeros((wide, lanes), f32)
        for z in range(RZONES):
            rate = jnp.where(cells[5, ext, :] == float(z), table_ref[r, z], rate)
        rates[r] = rate

    def pack(acc, v, slot):
        moved = pltpu.roll(v, lax.rem(slot - inner_lane + lanes, lanes), 1)
        return jnp.where(lane == slot, moved, acc)

    def unpack(stage, k, slot, span):
        return pltpu.roll(yrecv[stage, k, span, :], lax.rem(inner_lane - slot + lanes, lanes), 1)

    def enter(k):
        @pl.when(has_lo)
        def _():
            x_copy(k, 1).wait_recv()

        @pl.when(has_hi)
        def _():
            x_copy(k, 0).wait_recv()

        acc = pack(jnp.zeros((wide, lanes), f32), cells[1, ext, :], NC)
        acc = pack(acc, cells[3, ext, :], NC + 1)
        for c in range(NC):
            sta[k, c, BASE : BASE + rows, :] = inbuf[k, c]
            sta[k, c, BASE - HALO : BASE, :] = xrecv[k, 0, HALO * c : HALO * (c + 1), :]
            sta[k, c, BASE + rows : BASE + rows + HALO, :] = xrecv[k, 1, HALO * c : HALO * (c + 1), :]
            acc = pack(acc, sta[k, c, ext, :], c)
        ysend[0, k] = acc
        y_copy(0, k).start()

    def disperse(src, stage, which, k, start, count, put):
        y_copy(stage, k).wait_recv()
        inside = pl.ds(start - EXT, count)
        cut = slice(start - EXT, start - EXT + count)

        def near(c, kk):
            v = src[kk, c, start : start + count, :]
            sx = src[kk, c, start - 2 : start - 2 + count, :] + src[kk, c, start + 2 : start + 2 + count, :]
            return v, sx

        @pl.when(k == 0)
        def _():
            for c in range(NC):
                v, sx = near(c, 0)
                lap_y = (
                    jnp.where(first[cut], 0.0, pltpu.roll(v, 1, 1))
                    + jnp.where(last[cut], 0.0, pltpu.roll(v, lanes - 1, 1))
                    + jnp.where(inner[cut], unpack(stage, 0, c, inside), 0.0)
                    - 2.0 * v
                )
                part = DISP_STEP * valid[cut]
                extra_d[which, 1, c, inside, :] = part * cells[0, start : start + count, :] * (sx - 2.0 * v)
                extra_d[which, 2, c, inside, :] = part * cells[1, start : start + count, :] * lap_y

        index = jnp.where(k == 1, 1, jnp.where(k == 2, 2, 0))
        acc = jnp.zeros((count, lanes), f32)
        for c in range(NC):
            v, sx = near(c, k)
            other = jnp.where(
                even[cut],
                src[k, c, start + 1 : start + 1 + count, :],
                src[k, c, start - 1 : start - 1 + count, :],
            )
            out = (
                disp[0, c, inside, :] * v
                + disp[1, c, inside, :] * sx
                + disp[2, c, inside, :] * other
                + disp[3, c, inside, :] * pltpu.roll(v, 1, 1)
                + disp[4, c, inside, :] * pltpu.roll(v, lanes - 1, 1)
                + disp[5, c, inside, :] * unpack(stage, k, c, inside)
                + extra_d[which, index, c, inside, :]
            )
            put(k, c, out)
            if which == 0:
                acc = pack(acc, out, c)
        if which == 0:
            ysend[1, k] = acc
            y_copy(1, k).start()

    def put_stb(k, c, out):
        stb[k, c, ext, :] = out

    def put_out(k, c, out):
        outbuf[k, c] = out

    def advection_fields():
        keep = jnp.where(gy == 0, 1.0, 0.0)
        vx, vy, ux, uy = [cells[f, ext, :] for f in range(4)]
        ahead = pl.ds(EXT + 2, wide)
        vx_next = cells[0, ahead, :]
        ux_next = cells[2, ahead, :]
        shift = lambda slot: pltpu.roll(yrecv[0, 0], lanes - 1 - slot, 1)
        vy_next = jnp.where(last, shift(NC) * keep, pltpu.roll(vy, lanes - 1, 1))
        uy_next = jnp.where(last, shift(NC + 1) * keep, pltpu.roll(uy, lanes - 1, 1))
        ayl = vy * uy
        ayh = vy_next * (1.0 - uy_next)
        adv[0] = vx_next * ux_next + vx * (1.0 - ux) + vy_next * uy_next + vy * (1.0 - uy)
        adv[1] = vx * ux
        adv[2] = vx_next * (1.0 - ux_next)
        adv[3] = jnp.where(first, 0.0, ayl)
        adv[4] = jnp.where(last, 0.0, ayh)
        adv[5] = jnp.where(inner, keep * ayh + (1.0 - keep) * ayl, 0.0)

    def divergence(k, c):
        v = stb[k, c, ext, :]
        div = (
            adv[0] * v
            - adv[1] * stb[k, c, EXT - 2 : EXT - 2 + wide, :]
            - adv[2] * stb[k, c, EXT + 2 : EXT + 2 + wide, :]
            - adv[3] * pltpu.roll(v, 1, 1)
            - adv[4] * pltpu.roll(v, lanes - 1, 1)
            - adv[5] * unpack(1, k, c, slice(None))
        )
        return v, div

    def advect(k):
        y_copy(1, k).wait_recv()

        @pl.when(k == 0)
        def _():
            advection_fields()
            for c in range(NC):
                v, div = divergence(0, c)
                step = scale[c]
                extra_a[c] = div * (cap_ref[c] / COURANT) * step * step
                if c < 2 * NR:
                    state[c] = v - step * div

        here = cells[4, ext, :] == (k - 6).astype(f32)
        for c in range(NC):
            v, div = divergence(k, c)
            sta[k, c, ext, :] = v - scale[c] * div + jnp.where(here, extra_a[c], 0.0)

        half = jnp.where(k == 0, 0.5, 1.0)
        for start, count in ((0, 24), (24, wide - 24)):
            part = pl.ds(EXT + start, count)
            inside = pl.ds(start, count)
            v = [sta[k, c, part, :] for c in range(NC)]
            q = []
            for r in range(NR):
                donor = state[2 * r, inside, :]
                accept = state[2 * r + 1, inside, :]
                rate = rates[r, inside, :]
                flag = jnp.where(k == 3 + r, 1.0, 0.0)
                both = accept * v[2 * r] + donor * v[2 * r + 1]
                q.append(rate * ((p_ref[2 + r] * half) * both + flag * (donor * accept)))
            for c in range(NC):
                acc = exch_ref[c, 0] * v[0]
                for d in range(1, NC):
                    acc = acc + exch_ref[c, d] * v[d]
                for r in range(NR):
                    acc = acc + stoich_ref[r, c] * q[r]
                sta[k, c, part, :] = v[c] + REACT_STEP * acc

        acc = jnp.zeros((wide, lanes), f32)
        for c in range(NC):
            acc = pack(acc, sta[k, c, ext, :], c)
        ysend[2, k] = acc
        y_copy(2, k).start()

    def store_first():
        return pltpu.make_async_copy(outbuf.at[0], conc_out, store_sem.at[0])

    def store(k):
        return pltpu.make_async_copy(outbuf.at[k], sens_out.at[k - 1], store_sem.at[k])

    def leave(k):
        disperse(sta, 2, 1, k, BASE, rows, put_out)

        @pl.when(k == 0)
        def _():
            store_first().start()

        @pl.when(k > 0)
        def _():
            store(k).start()

    def turn(t, carry):
        @pl.when(t < NK)
        def _():
            enter(t)

        @pl.when(jnp.logical_and(t >= 1, t < NK + 1))
        def _():
            disperse(sta, 0, 0, t - 1, EXT, wide, put_stb)

        @pl.when(jnp.logical_and(t >= 2, t < NK + 2))
        def _():
            advect(t - 2)

        @pl.when(t >= 3)
        def _():
            leave(t - 3)

        return carry

    lax.fori_loop(0, NK + 3, turn, 0)

    def finish(k, carry):
        for stage in range(3):
            y_copy(stage, k).wait_send()

        @pl.when(has_lo)
        def _():
            x_copy(k, 0).wait_send()

        @pl.when(has_hi)
        def _():
            x_copy(k, 1).wait_send()

        return carry

    lax.fori_loop(0, NK, finish, 0)

    @pl.when(has_lo)
    def _():
        f_copy(0).wait_send()

    @pl.when(has_hi)
    def _():
        f_copy(1).wait_send()

    store_first().wait()
    for k in range(1, NK):
        store(k).wait()


def on_device(
    conc,
    sens,
    vel_x,
    vel_y,
    up_x,
    up_y,
    sorb_zone,
    rate_zone,
    param_values,
    mol_diff,
    sorb_cap,
    rate_table,
    exch_matrix,
    stoich,
):
    nx, layers, ny = vel_x.shape
    rows = nx * layers
    wide = rows + 2 * (BASE - EXT)
    tall = rows + 2 * BASE
    flat = lambda a: a.reshape(a.shape[:-3] + (rows, ny))
    vmem = pl.BlockSpec(memory_space=pltpu.VMEM)
    smem = pl.BlockSpec(memory_space=pltpu.SMEM)
    hbm = pl.BlockSpec(memory_space=pl.ANY)
    f32 = jnp.float32
    dma = pltpu.SemaphoreType.DMA
    conc_out, sens_out = pl.pallas_call(
        functools.partial(kernel, rows, ny),
        out_shape=(
            jax.ShapeDtypeStruct((NC, rows, ny), f32),
            jax.ShapeDtypeStruct((NP, NC, rows, ny), f32),
        ),
        in_specs=[hbm, hbm] + [vmem] * 6 + [smem] * 6,
        out_specs=(hbm, hbm),
        scratch_shapes=[
            pltpu.VMEM((NK, NC, rows, ny), f32),
            pltpu.VMEM((NK, NC, rows, ny), f32),
            pltpu.VMEM((NK, NC, tall, ny), f32),
            pltpu.VMEM((NK, NC, tall, ny), f32),
            pltpu.VMEM((NK, 2, HALO * NC, ny), f32),
            pltpu.VMEM((NK, 2, HALO * NC, ny), f32),
            pltpu.VMEM((3, NK, wide, ny), f32),
            pltpu.VMEM((3, NK, wide, ny), f32),
            pltpu.VMEM((2, 40, ny), f32),
            pltpu.VMEM((2, 40, ny), f32),
            pltpu.VMEM((6, tall, ny), f32),
            pltpu.VMEM((6, NC, wide, ny), f32),
            pltpu.VMEM((6, wide, ny), f32),
            pltpu.VMEM((NC, wide, ny), f32),
            pltpu.VMEM((NR, wide, ny), f32),
            pltpu.VMEM((2 * NR, wide, ny), f32),
            pltpu.VMEM((2, 3, NC, wide, ny), f32),
            pltpu.VMEM((NC, wide, ny), f32),
            dma((NK,)),
            dma((NK,)),
            dma((NK, 2)),
            dma((NK, 2)),
            dma((3, NK)),
            dma((3, NK)),
            dma((2,)),
            dma((2,)),
        ],
        compiler_params=pltpu.CompilerParams(
            collective_id=0, has_side_effects=True, vmem_limit_bytes=62 * 1024 * 1024
        ),
    )(
        flat(conc),
        flat(sens),
        flat(vel_x),
        flat(vel_y),
        flat(up_x),
        flat(up_y),
        flat(sorb_zone),
        flat(rate_zone),
        param_values,
        mol_diff,
        sorb_cap,
        jnp.transpose(rate_table),
        exch_matrix,
        jnp.transpose(stoich),
    )
    return conc_out.reshape(conc.shape), sens_out.reshape(sens.shape)


def solution(mesh):
    cell = P(("parts", "gx"), None, "gy")
    outs = (P(None, ("parts", "gx"), None, "gy"), P(None, None, ("parts", "gx"), None, "gy"))
    return jax.shard_map(
        on_device,
        mesh=mesh,
        in_specs=outs + (cell,) * 6 + (P(),) * 6,
        out_specs=outs,
        check_vma=False,
    )
```

time: 38.9 us -> 38.6 us (level)
  the two profiles are of different devices: /device:TPU:17 before, /device:TPU:11 now
where the time goes in v1:
time: 38.6 us; the launch traced here: 38.4 us
  Pallas kernels  33.4 us (87%)
  local copies, waits for them, and re-layouts  4.28 us (11%)
  between operations  0.64 us (2%)
    pallas_call x1, Pallas kernels, on_device(): pl.pallas_call(functools.partial(kernel, rows, ny), out_shape=(jax.ShapeD...  33.4 us
    unnamed x2, local copies, waits for them, and re-layouts  4.28 us

profile of v1, /device:TPU:11, one launch (start us, length us, event | category | flops | bytes accessed | tf_op | source)
XLA Modules:
  0.0 38.4 jit_solution(5943454930075821994)
XLA Ops:
  0.6 33.4 %shard_map.149 = (f32[12,32,128]{2,1,0:T(8,128)}, f32[8,12,32,128]{3,2,1,0:T(8,128)}) custom-call(f32[12,32,128]{2,1,0:T(8,128)} %bitcast.15, f32[8,12,32,128]{3,2,1,0:T(8,128)} %bitcast.13, f32[32,128]{1,0:T(8,128)} %bitcast.16, f32[32,128]{1,0:T(8,128)} %bitcast.17, s32[32,128]{1,0:T(8,128)} %bitcast.18, s32[32,128]{1,0:T(8,128)} %bitcast.19, ...), custom_call_target="tpu_custom_call" | custom-call | tf_op jit(solution)/shard_map/pallas_call | solution.py:485
  34.1 1.6 %copy.18 = f32[12,16,2,128]{3,2,1,0:T(2,128)} copy(f32[12,16,2,128]{3,2,1,0:T(2,128)} %bitcast.14) | data formatting | bytes 393216
  35.7 2.7 %copy.19 = f32[8,12,16,2,128]{4,3,2,1,0:T(2,128)} copy(f32[8,12,16,2,128]{4,3,2,1,0:T(2,128)} %bitcast.12) | data formatting | bytes 3145728

commit v2 on v1

--- a/solution.py
+++ b/solution.py
@@ -20,6 +20,7 @@
 BASE = 12
 EXT = 8
 HALO = 6
+AHEAD = 3
 
 
 def kernel(
@@ -45,12 +46,13 @@
     outbuf,
     sta,
     stb,
+    stc,
     xsend,
     xrecv,
-    ysend,
     yrecv,
     fsend,
     frecv,
+    yfields,
     cells,
     disp,
     adv,
@@ -67,6 +69,8 @@
     yr_sem,
     fs_sem,
     fr_sem,
+    yfs_sem,
+    yfr_sem,
 ):
     gx = lax.axis_index("gx")
     gy = lax.axis_index("gy")
@@ -136,15 +140,25 @@
             device_id={"gx": gx - 1 if side == 0 else gx + 1},
         )
 
+    ext = pl.ds(EXT, wide)
+
     def y_copy(stage, k):
         return pltpu.make_async_remote_copy(
-            src_ref=ysend.at[stage, k],
+            src_ref=(sta, stb, stc)[stage].at[k, :, ext, :],
             dst_ref=yrecv.at[stage, k],
             send_sem=ys_sem.at[stage, k],
             recv_sem=yr_sem.at[stage, k],
             device_id={"gy": 1 - gy},
         )
 
+    yf_copy = pltpu.make_async_remote_copy(
+        src_ref=cells.at[:, ext, :],
+        dst_ref=yfields,
+        send_sem=yfs_sem,
+        recv_sem=yfr_sem,
+        device_id={"gy": 1 - gy},
+    )
+
     count = 1 + has_lo.astype(jnp.int32) + has_hi.astype(jnp.int32)
     pl.semaphore_wait(barrier, count)
 
@@ -177,7 +191,7 @@
         send(k)
         return carry
 
-    lax.fori_loop(1, NK, send_step, 0)
+    lax.fori_loop(1, AHEAD, send_step, 0)
 
     @pl.when(has_lo)
     def _():
@@ -191,19 +205,21 @@
         cells[f, BASE - HALO : BASE, :] = frecv[0, HALO * f : HALO * (f + 1), :]
         cells[f, BASE + rows : BASE + rows + HALO, :] = frecv[1, HALO * f : HALO * (f + 1), :]
 
+    yf_copy.start()
+
     lane = lax.broadcasted_iota(jnp.int32, (wide, lanes), 1)
     row = lax.broadcasted_iota(jnp.int32, (wide, lanes), 0)
     even = (row % 2) == 0
-    inner_lane = jnp.where(gy == 0, lanes - 1, 0)
     first = lane == 0
     last = lane == lanes - 1
-    inner = lane == inner_lane
+    no_lo = jnp.logical_and(first, gy == 0)
+    no_hi = jnp.logical_and(last, gy == 1)
+    from_lo = jnp.logical_and(last, gy == 1)
+    from_hi = jnp.logical_and(first, gy == 0)
     margin = BASE - EXT
     lo_ok = jnp.where(has_lo, 1.0, 0.0)
     hi_ok = jnp.where(has_hi, 1.0, 0.0)
     valid = jnp.where(row < margin, lo_ok, jnp.where(row >= margin + rows, hi_ok, 1.0))
-    ext = pl.ds(EXT, wide)
-
     fx = DISP_STEP * p_ref[0] * cells[0, ext, :]
     fy = DISP_STEP * p_ref[1] * cells[1, ext, :]
     sorb = jnp.zeros((wide, lanes), f32)
@@ -218,9 +234,8 @@
         disp[0, c] = valid - 2.0 * cx - 2.0 * cy - cm
         disp[1, c] = cx
         disp[2, c] = cm
-        disp[3, c] = jnp.where(first, 0.0, cy)
-        disp[4, c] = jnp.where(last, 0.0, cy)
-        disp[5, c] = jnp.where(inner, cy, 0.0)
+        disp[3, c] = jnp.where(no_lo, 0.0, cy)
+        disp[4, c] = jnp.where(no_hi, 0.0, cy)
         scale[c] = valid * COURANT / (1.0 + sorb * cap_ref[c])
         for stage in range(2):
             extra_d[stage, 0, c] = jnp.zeros((wide, lanes), f32)
@@ -233,12 +248,11 @@
             rate = jnp.where(cells[5, ext, :] == float(z), table_ref[r, z], rate)
         rates[r] = rate
 
-    def pack(acc, v, slot):
-        moved = pltpu.roll(v, lax.rem(slot - inner_lane + lanes, lanes), 1)
-        return jnp.where(lane == slot, moved, acc)
-
-    def unpack(stage, k, slot, span):
-        return pltpu.roll(yrecv[stage, k, span, :], lax.rem(inner_lane - slot + lanes, lanes), 1)
+    def y_near(v, stage, k, c, span, cut):
+        other = yrecv[stage, k, c, span, :]
+        low = pltpu.roll(jnp.where(from_lo[cut], other, v), 1, 1)
+        high = pltpu.roll(jnp.where(from_hi[cut], other, v), lanes - 1, 1)
+        return low, high
 
     def enter(k):
         @pl.when(has_lo)
@@ -249,15 +263,16 @@
         def _():
             x_copy(k, 0).wait_recv()
 
-        acc = pack(jnp.zeros((wide, lanes), f32), cells[1, ext, :], NC)
-        acc = pack(acc, cells[3, ext, :], NC + 1)
         for c in range(NC):
             sta[k, c, BASE : BASE + rows, :] = inbuf[k, c]
             sta[k, c, BASE - HALO : BASE, :] = xrecv[k, 0, HALO * c : HALO * (c + 1), :]
             sta[k, c, BASE + rows : BASE + rows + HALO, :] = xrecv[k, 1, HALO * c : HALO * (c + 1), :]
-            acc = pack(acc, sta[k, c, ext, :], c)
-        ysend[0, k] = acc
         y_copy(0, k).start()
+
+        @pl.when(k + AHEAD < NK)
+        def _():
+            load(k + AHEAD).wait()
+            send(k + AHEAD)
 
     def disperse(src, stage, which, k, start, count, put):
         y_copy(stage, k).wait_recv()
@@ -273,20 +288,16 @@
         def _():
             for c in range(NC):
                 v, sx = near(c, 0)
-                lap_y = (
-                    jnp.where(first[cut], 0.0, pltpu.roll(v, 1, 1))
-                    + jnp.where(last[cut], 0.0, pltpu.roll(v, lanes - 1, 1))
-                    + jnp.where(inner[cut], unpack(stage, 0, c, inside), 0.0)
-                    - 2.0 * v
-                )
+                yl, yh = y_near(v, stage, 0, c, inside, cut)
+                lap_y = jnp.where(no_lo[cut], 0.0, yl) + jnp.where(no_hi[cut], 0.0, yh) - 2.0 * v
                 part = DISP_STEP * valid[cut]
                 extra_d[which, 1, c, inside, :] = part * cells[0, start : start + count, :] * (sx - 2.0 * v)
                 extra_d[which, 2, c, inside, :] = part * cells[1, start : start + count, :] * lap_y
 
         index = jnp.where(k == 1, 1, jnp.where(k == 2, 2, 0))
-        acc = jnp.zeros((count, lanes), f32)
         for c in range(NC):
             v, sx = near(c, k)
+            yl, yh = y_near(v, stage, k, c, inside, cut)
             other = jnp.where(
                 even[cut],
                 src[k, c, start + 1 : start + 1 + count, :],
@@ -296,16 +307,12 @@
                 disp[0, c, inside, :] * v
                 + disp[1, c, inside, :] * sx
                 + disp[2, c, inside, :] * other
-                + disp[3, c, inside, :] * pltpu.roll(v, 1, 1)
-                + disp[4, c, inside, :] * pltpu.roll(v, lanes - 1, 1)
-                + disp[5, c, inside, :] * unpack(stage, k, c, inside)
+                + disp[3, c, inside, :] * yl
+                + disp[4, c, inside, :] * yh
                 + extra_d[which, index, c, inside, :]
             )
             put(k, c, out)
-            if which == 0:
-                acc = pack(acc, out, c)
         if which == 0:
-            ysend[1, k] = acc
             y_copy(1, k).start()
 
     def put_stb(k, c, out):
@@ -320,27 +327,26 @@
         ahead = pl.ds(EXT + 2, wide)
         vx_next = cells[0, ahead, :]
         ux_next = cells[2, ahead, :]
-        shift = lambda slot: pltpu.roll(yrecv[0, 0], lanes - 1 - slot, 1)
-        vy_next = jnp.where(last, shift(NC) * keep, pltpu.roll(vy, lanes - 1, 1))
-        uy_next = jnp.where(last, shift(NC + 1) * keep, pltpu.roll(uy, lanes - 1, 1))
+        yf_copy.wait_recv()
+        vy_next = jnp.where(last, keep, 1.0) * pltpu.roll(jnp.where(from_hi, yfields[1], vy), lanes - 1, 1)
+        uy_next = jnp.where(last, keep, 1.0) * pltpu.roll(jnp.where(from_hi, yfields[3], uy), lanes - 1, 1)
         ayl = vy * uy
         ayh = vy_next * (1.0 - uy_next)
         adv[0] = vx_next * ux_next + vx * (1.0 - ux) + vy_next * uy_next + vy * (1.0 - uy)
         adv[1] = vx * ux
         adv[2] = vx_next * (1.0 - ux_next)
-        adv[3] = jnp.where(first, 0.0, ayl)
-        adv[4] = jnp.where(last, 0.0, ayh)
-        adv[5] = jnp.where(inner, keep * ayh + (1.0 - keep) * ayl, 0.0)
+        adv[3] = jnp.where(no_lo, 0.0, ayl)
+        adv[4] = jnp.where(no_hi, 0.0, ayh)
 
     def divergence(k, c):
         v = stb[k, c, ext, :]
+        yl, yh = y_near(v, 1, k, c, slice(None), slice(None))
         div = (
             adv[0] * v
             - adv[1] * stb[k, c, EXT - 2 : EXT - 2 + wide, :]
             - adv[2] * stb[k, c, EXT + 2 : EXT + 2 + wide, :]
-            - adv[3] * pltpu.roll(v, 1, 1)
-            - adv[4] * pltpu.roll(v, lanes - 1, 1)
-            - adv[5] * unpack(1, k, c, slice(None))
+            - adv[3] * yl
+            - adv[4] * yh
         )
         return v, div
 
@@ -360,13 +366,13 @@
         here = cells[4, ext, :] == (k - 6).astype(f32)
         for c in range(NC):
             v, div = divergence(k, c)
-            sta[k, c, ext, :] = v - scale[c] * div + jnp.where(here, extra_a[c], 0.0)
+            stc[k, c, ext, :] = v - scale[c] * div + jnp.where(here, extra_a[c], 0.0)
 
         half = jnp.where(k == 0, 0.5, 1.0)
         for start, count in ((0, 24), (24, wide - 24)):
             part = pl.ds(EXT + start, count)
             inside = pl.ds(start, count)
-            v = [sta[k, c, part, :] for c in range(NC)]
+            v = [stc[k, c, part, :] for c in range(NC)]
             q = []
             for r in range(NR):
                 donor = state[2 * r, inside, :]
@@ -381,12 +387,8 @@
                     acc = acc + exch_ref[c, d] * v[d]
                 for r in range(NR):
                     acc = acc + stoich_ref[r, c] * q[r]
-                sta[k, c, part, :] = v[c] + REACT_STEP * acc
-
-        acc = jnp.zeros((wide, lanes), f32)
-        for c in range(NC):
-            acc = pack(acc, sta[k, c, ext, :], c)
-        ysend[2, k] = acc
+                stc[k, c, part, :] = v[c] + REACT_STEP * acc
+
         y_copy(2, k).start()
 
     def store_first():
@@ -396,7 +398,7 @@
         return pltpu.make_async_copy(outbuf.at[k], sens_out.at[k - 1], store_sem.at[k])
 
     def leave(k):
-        disperse(sta, 2, 1, k, BASE, rows, put_out)
+        disperse(stc, 2, 1, k, BASE, rows, put_out)
 
         @pl.when(k == 0)
         def _():
@@ -442,6 +444,7 @@
         return carry
 
     lax.fori_loop(0, NK, finish, 0)
+    yf_copy.wait_send()
 
     @pl.when(has_lo)
     def _():
@@ -495,15 +498,16 @@
             pltpu.VMEM((NK, NC, rows, ny), f32),
             pltpu.VMEM((NK, NC, tall, ny), f32),
             pltpu.VMEM((NK, NC, tall, ny), f32),
+            pltpu.VMEM((NK, NC, tall, ny), f32),
             pltpu.VMEM((NK, 2, HALO * NC, ny), f32),
             pltpu.VMEM((NK, 2, HALO * NC, ny), f32),
-            pltpu.VMEM((3, NK, wide, ny), f32),
-            pltpu.VMEM((3, NK, wide, ny), f32),
+            pltpu.VMEM((3, NK, NC, wide, ny), f32),
             pltpu.VMEM((2, 40, ny), f32),
             pltpu.VMEM((2, 40, ny), f32),
+            pltpu.VMEM((6, wide, ny), f32),
             pltpu.VMEM((6, tall, ny), f32),
-            pltpu.VMEM((6, NC, wide, ny), f32),
-            pltpu.VMEM((6, wide, ny), f32),
+            pltpu.VMEM((5, NC, wide, ny), f32),
+            pltpu.VMEM((5, wide, ny), f32),
             pltpu.VMEM((NC, wide, ny), f32),
             pltpu.VMEM((NR, wide, ny), f32),
             pltpu.VMEM((2 * NR, wide, ny), f32),
@@ -517,6 +521,8 @@
             dma((3, NK)),
             dma((2,)),
             dma((2,)),
+            dma,
+            dma,
         ],
         compiler_params=pltpu.CompilerParams(
             collective_id=0, has_side_effects=True, vmem_limit_bytes=62 * 1024 * 1024

time: 38.6 us -> 33.4 us (0.87)
  Pallas kernels: 33.4 us -> 28.1 us
    pallas_call x1, Pallas kernels: 33.4 us -> 28.1 us  [on_device(): pl.pallas_call(functools.partial(kernel, rows, ny), out_shape=(jax.ShapeD...]
where the time goes in v2:
time: 33.4 us; the launch traced here: 33 us
  Pallas kernels  28.1 us (84%)
  local copies, waits for them, and re-layouts  4.28 us (13%)
  between operations  0.64 us (2%)
    pallas_call x1, Pallas kernels, on_device(): pl.pallas_call(functools.partial(kernel, rows, ny), out_shape=(jax.ShapeD...  28.1 us
    unnamed x2, local copies, waits for them, and re-layouts  4.28 us

profile of v2, /device:TPU:11, one launch (start us, length us, event | category | flops | bytes accessed | tf_op | source)
XLA Modules:
  0.0 33.0 jit_solution(16108827490717410142)
XLA Ops:
  0.6 28.1 %shard_map.149 = (f32[12,32,128]{2,1,0:T(8,128)}, f32[8,12,32,128]{3,2,1,0:T(8,128)}) custom-call(f32[12,32,128]{2,1,0:T(8,128)} %bitcast.15, f32[8,12,32,128]{3,2,1,0:T(8,128)} %bitcast.13, f32[32,128]{1,0:T(8,128)} %bitcast.16, f32[32,128]{1,0:T(8,128)} %bitcast.17, s32[32,128]{1,0:T(8,128)} %bitcast.18, s32[32,128]{1,0:T(8,128)} %bitcast.19, ...), custom_call_target="tpu_custom_call" | custom-call | tf_op jit(solution)/shard_map/pallas_call | solution.py:488
  28.8 1.6 %copy.18 = f32[12,16,2,128]{3,2,1,0:T(2,128)} copy(f32[12,16,2,128]{3,2,1,0:T(2,128)} %bitcast.14) | data formatting | bytes 393216
  30.4 2.7 %copy.19 = f32[8,12,16,2,128]{4,3,2,1,0:T(2,128)} copy(f32[8,12,16,2,128]{4,3,2,1,0:T(2,128)} %bitcast.12) | data formatting | bytes 3145728

commit v3 on v2

--- a/solution.py
+++ b/solution.py
@@ -49,6 +49,7 @@
     stc,
     xsend,
     xrecv,
+    ysend,
     yrecv,
     fsend,
     frecv,
@@ -144,7 +145,7 @@
 
     def y_copy(stage, k):
         return pltpu.make_async_remote_copy(
-            src_ref=(sta, stb, stc)[stage].at[k, :, ext, :],
+            src_ref=ysend.at[stage, k],
             dst_ref=yrecv.at[stage, k],
             send_sem=ys_sem.at[stage, k],
             recv_sem=yr_sem.at[stage, k],
@@ -212,6 +213,7 @@
     even = (row % 2) == 0
     first = lane == 0
     last = lane == lanes - 1
+    sent = jnp.where(gy == 0, lanes - 1, 0)
     no_lo = jnp.logical_and(first, gy == 0)
     no_hi = jnp.logical_and(last, gy == 1)
     from_lo = jnp.logical_and(last, gy == 1)
@@ -248,8 +250,14 @@
             rate = jnp.where(cells[5, ext, :] == float(z), table_ref[r, z], rate)
         rates[r] = rate
 
+    def pack(acc, v, c):
+        moved = pltpu.roll(v, c, 1) if c > 0 else v
+        return jnp.where(lane == lax.rem(sent + c, lanes), moved, acc)
+
     def y_near(v, stage, k, c, span, cut):
-        other = yrecv[stage, k, c, span, :]
+        other = yrecv[stage, k, span, :]
+        if c > 0:
+            other = pltpu.roll(other, lanes - c, 1)
         low = pltpu.roll(jnp.where(from_lo[cut], other, v), 1, 1)
         high = pltpu.roll(jnp.where(from_hi[cut], other, v), lanes - 1, 1)
         return low, high
@@ -263,10 +271,13 @@
         def _():
             x_copy(k, 0).wait_recv()
 
+        acc = jnp.zeros((wide, lanes), f32)
         for c in range(NC):
             sta[k, c, BASE : BASE + rows, :] = inbuf[k, c]
             sta[k, c, BASE - HALO : BASE, :] = xrecv[k, 0, HALO * c : HALO * (c + 1), :]
             sta[k, c, BASE + rows : BASE + rows + HALO, :] = xrecv[k, 1, HALO * c : HALO * (c + 1), :]
+            acc = pack(acc, sta[k, c, ext, :], c)
+        ysend[0, k] = acc
         y_copy(0, k).start()
 
         @pl.when(k + AHEAD < NK)
@@ -295,6 +306,7 @@
                 extra_d[which, 2, c, inside, :] = part * cells[1, start : start + count, :] * lap_y
 
         index = jnp.where(k == 1, 1, jnp.where(k == 2, 2, 0))
+        acc = jnp.zeros((count, lanes), f32)
         for c in range(NC):
             v, sx = near(c, k)
             yl, yh = y_near(v, stage, k, c, inside, cut)
@@ -312,7 +324,10 @@
                 + extra_d[which, index, c, inside, :]
             )
             put(k, c, out)
+            if which == 0:
+                acc = pack(acc, out, c)
         if which == 0:
+            ysend[1, k] = acc
             y_copy(1, k).start()
 
     def put_stb(k, c, out):
@@ -389,6 +404,10 @@
                     acc = acc + stoich_ref[r, c] * q[r]
                 stc[k, c, part, :] = v[c] + REACT_STEP * acc
 
+        acc = jnp.zeros((wide, lanes), f32)
+        for c in range(NC):
+            acc = pack(acc, stc[k, c, ext, :], c)
+        ysend[2, k] = acc
         y_copy(2, k).start()
 
     def store_first():
@@ -501,7 +520,8 @@
             pltpu.VMEM((NK, NC, tall, ny), f32),
             pltpu.VMEM((NK, 2, HALO * NC, ny), f32),
             pltpu.VMEM((NK, 2, HALO * NC, ny), f32),
-            pltpu.VMEM((3, NK, NC, wide, ny), f32),
+            pltpu.VMEM((3, NK, wide, ny), f32),
+            pltpu.VMEM((3, NK, wide, ny), f32),
             pltpu.VMEM((2, 40, ny), f32),
             pltpu.VMEM((2, 40, ny), f32),
             pltpu.VMEM((6, wide, ny), f32),

time: 33.4 us -> 35.4 us (1.060)
  Pallas kernels: 28.1 us -> 30.2 us
    pallas_call x1, Pallas kernels: 28.1 us -> 30.2 us  [on_device(): pl.pallas_call(functools.partial(kernel, rows, ny), out_shape=(jax.ShapeD...]
where the time goes in v3:
time: 35.4 us; the launch traced here: 35.1 us
  Pallas kernels  30.2 us (85%)
  local copies, waits for them, and re-layouts  4.28 us (12%)
  between operations  0.64 us (2%)
    pallas_call x1, Pallas kernels, on_device(): pl.pallas_call(functools.partial(kernel, rows, ny), out_shape=(jax.ShapeD...  30.2 us
    unnamed x2, local copies, waits for them, and re-layouts  4.28 us

profile of v3, /device:TPU:11, one launch (start us, length us, event | category | flops | bytes accessed | tf_op | source)
XLA Modules:
  0.0 35.1 jit_solution(10646958614608916079)
XLA Ops:
  0.6 30.2 %shard_map.149 = (f32[12,32,128]{2,1,0:T(8,128)}, f32[8,12,32,128]{3,2,1,0:T(8,128)}) custom-call(f32[12,32,128]{2,1,0:T(8,128)} %bitcast.15, f32[8,12,32,128]{3,2,1,0:T(8,128)} %bitcast.13, f32[32,128]{1,0:T(8,128)} %bitcast.16, f32[32,128]{1,0:T(8,128)} %bitcast.17, s32[32,128]{1,0:T(8,128)} %bitcast.18, s32[32,128]{1,0:T(8,128)} %bitcast.19, ...), custom_call_target="tpu_custom_call" | custom-call | tf_op jit(solution)/shard_map/pallas_call | solution.py:507
  30.8 1.6 %copy.18 = f32[12,16,2,128]{3,2,1,0:T(2,128)} copy(f32[12,16,2,128]{3,2,1,0:T(2,128)} %bitcast.14) | data formatting | bytes 393216
  32.4 2.7 %copy.19 = f32[8,12,16,2,128]{4,3,2,1,0:T(2,128)} copy(f32[8,12,16,2,128]{4,3,2,1,0:T(2,128)} %bitcast.12) | data formatting | bytes 3145728

commit v4 on v2

--- a/solution.py
+++ b/solution.py
@@ -49,6 +49,8 @@
     stc,
     xsend,
     xrecv,
+    ysend,
+    ypack,
     yrecv,
     fsend,
     frecv,
@@ -144,8 +146,8 @@
 
     def y_copy(stage, k):
         return pltpu.make_async_remote_copy(
-            src_ref=(sta, stb, stc)[stage].at[k, :, ext, :],
-            dst_ref=yrecv.at[stage, k],
+            src_ref=ysend.at[k] if stage == 0 else (stb, stc)[stage - 1].at[k, :, ext, :],
+            dst_ref=ypack.at[k] if stage == 0 else yrecv.at[stage - 1, k],
             send_sem=ys_sem.at[stage, k],
             recv_sem=yr_sem.at[stage, k],
             device_id={"gy": 1 - gy},
@@ -212,6 +214,7 @@
     even = (row % 2) == 0
     first = lane == 0
     last = lane == lanes - 1
+    sent = jnp.where(gy == 0, lanes - 1, 0)
     no_lo = jnp.logical_and(first, gy == 0)
     no_hi = jnp.logical_and(last, gy == 1)
     from_lo = jnp.logical_and(last, gy == 1)
@@ -248,8 +251,17 @@
             rate = jnp.where(cells[5, ext, :] == float(z), table_ref[r, z], rate)
         rates[r] = rate
 
+    def pack(acc, v, c):
+        moved = pltpu.roll(v, c, 1) if c > 0 else v
+        return jnp.where(lane == lax.rem(sent + c, lanes), moved, acc)
+
     def y_near(v, stage, k, c, span, cut):
-        other = yrecv[stage, k, c, span, :]
+        if stage == 0:
+            other = ypack[k, span, :]
+            if c > 0:
+                other = pltpu.roll(other, lanes - c, 1)
+        else:
+            other = yrecv[stage - 1, k, c, span, :]
         low = pltpu.roll(jnp.where(from_lo[cut], other, v), 1, 1)
         high = pltpu.roll(jnp.where(from_hi[cut], other, v), lanes - 1, 1)
         return low, high
@@ -263,10 +275,13 @@
         def _():
             x_copy(k, 0).wait_recv()
 
+        acc = jnp.zeros((wide, lanes), f32)
         for c in range(NC):
             sta[k, c, BASE : BASE + rows, :] = inbuf[k, c]
             sta[k, c, BASE - HALO : BASE, :] = xrecv[k, 0, HALO * c : HALO * (c + 1), :]
             sta[k, c, BASE + rows : BASE + rows + HALO, :] = xrecv[k, 1, HALO * c : HALO * (c + 1), :]
+            acc = pack(acc, sta[k, c, ext, :], c)
+        ysend[k] = acc
         y_copy(0, k).start()
 
         @pl.when(k + AHEAD < NK)
@@ -501,7 +516,9 @@
             pltpu.VMEM((NK, NC, tall, ny), f32),
             pltpu.VMEM((NK, 2, HALO * NC, ny), f32),
             pltpu.VMEM((NK, 2, HALO * NC, ny), f32),
-            pltpu.VMEM((3, NK, NC, wide, ny), f32),
+            pltpu.VMEM((NK, wide, ny), f32),
+            pltpu.VMEM((NK, wide, ny), f32),
+            pltpu.VMEM((2, NK, NC, wide, ny), f32),
             pltpu.VMEM((2, 40, ny), f32),
             pltpu.VMEM((2, 40, ny), f32),
             pltpu.VMEM((6, wide, ny), f32),

time: 33.4 us -> 33.6 us (level)
  no operation moved by 1% of the time
where the time goes in v4:
time: 33.6 us; the launch traced here: 33.1 us
  Pallas kernels  28.2 us (84%)
  local copies, waits for them, and re-layouts  4.28 us (13%)
  between operations  0.64 us (2%)
    pallas_call x1, Pallas kernels, on_device(): pl.pallas_call(functools.partial(kernel, rows, ny), out_shape=(jax.ShapeD...  28.2 us
    unnamed x2, local copies, waits for them, and re-layouts  4.28 us

profile of v4, /device:TPU:11, one launch (start us, length us, event | category | flops | bytes accessed | tf_op | source)
XLA Modules:
  0.0 33.1 jit_solution(10610659971373128494)
XLA Ops:
  0.6 28.2 %shard_map.149 = (f32[12,32,128]{2,1,0:T(8,128)}, f32[8,12,32,128]{3,2,1,0:T(8,128)}) custom-call(f32[12,32,128]{2,1,0:T(8,128)} %bitcast.15, f32[8,12,32,128]{3,2,1,0:T(8,128)} %bitcast.13, f32[32,128]{1,0:T(8,128)} %bitcast.16, f32[32,128]{1,0:T(8,128)} %bitcast.17, s32[32,128]{1,0:T(8,128)} %bitcast.18, s32[32,128]{1,0:T(8,128)} %bitcast.19, ...), custom_call_target="tpu_custom_call" | custom-call | tf_op jit(solution)/shard_map/pallas_call | solution.py:503
  28.8 1.6 %copy.18 = f32[12,16,2,128]{3,2,1,0:T(2,128)} copy(f32[12,16,2,128]{3,2,1,0:T(2,128)} %bitcast.14) | data formatting | bytes 393216
  30.4 2.7 %copy.19 = f32[8,12,16,2,128]{4,3,2,1,0:T(2,128)} copy(f32[8,12,16,2,128]{4,3,2,1,0:T(2,128)} %bitcast.12) | data formatting | bytes 3145728
